TPU v7x, 512 devices: a whole 4x4x16 slice. The times are simulated.
512 devices in a mesh: blk: 32 (over y_lo, z), gather: 16 (over y_hi, x, core).
Axes of the slice: x: 4, y: 4 (y_hi: 2, y_lo: 2; y = y_hi * 2 + y_lo), z: 16, core: 2. Of those that a mesh axis runs over, the one named last changes fastest.
Arguments:
- images: bfloat16 [65536, 1152], P(('blk', 'gather')), may hold values from -0.1796875 to 0.1796875
- captions: bfloat16 [65536, 1152], P(('blk', 'gather')), may hold values from -0.1796875 to 0.1796875
- pair_index: int32 [32, 2048], P('blk', 'gather'), may hold values from 0 to 2047, each once within a row
- logit_scale: float32 [1], replicated, may hold values from 1.5 to 2.5
- logit_bias: float32 [1], replicated, may hold values from -4 to -1
Outputs:
- loss_mean: float32 [1], replicated
- grad_images: float32 [65536, 1152], P(('blk', 'gather'))
- grad_captions: float32 [65536, 1152], P(('blk', 'gather'))
- grad_scale: float32 [1], replicated
- grad_bias: float32 [1], replicated
Inputs may be any that keep to these rules, and one draw needn't show every extreme that they name: Each row of pair_index is a permutation of 0 to 2047.
All inputs are finite; a program needn't handle non-finite values.
Results may differ from a plain program's by a relative error of at most 0.00075.
Values may be sent and summed in bfloat16 or wider, within the bound.
A program may use at most 64 MiB of HBM per device.

v0:
```python
import jax
import jax.numpy as jnp
from jax import lax
from jax.sharding import PartitionSpec as P

WINDOW = 2


EPS = 1e-06


def passed_along(block, axis, distance):
    devices = range(lax.axis_size(axis))
    route = [((i - distance) % len(devices), i) for i in devices]
    return lax.ppermute(block, axis, route)


def normalize(embedded):
    widened = embedded.astype(jnp.float32)
    inverse = lax.rsqrt(jnp.sum(widened * widened, axis=-1, keepdims=True) + EPS)
    return (widened * inverse, inverse)


def backnorm(unit, inverse, upstream):
    return inverse * (upstream - unit * jnp.sum(unit * upstream, axis=-1, keepdims=True))


def pair_terms(queries, keys, temper, offset, paired):
    sims = lax.dot_general(
        queries, keys, (((1,), (1,)), ((), ())), preferred_element_type=jnp.float32
    )
    logits = temper * sims + offset
    label = paired.astype(jnp.float32)
    loss_part = jnp.sum(jax.nn.softplus(-(2.0 * label - 1.0) * logits))
    coeff = jax.nn.sigmoid(logits) - label
    return (loss_part, jnp.sum(coeff * temper * sims), jnp.sum(coeff), coeff.astype(jnp.bfloat16))


def key_partial(coeff_low, queries):
    return lax.dot_general(
        coeff_low, queries, (((0,), (0,)), ((), ())), preferred_element_type=jnp.float32
    )


def on_device(images, captions, pair_index, logit_scale, logit_bias):
    unit_img, inv_img = normalize(images)
    unit_cap, inv_cap = normalize(captions)
    queries = unit_img.astype(jnp.bfloat16)
    own_keys = unit_cap.astype(jnp.bfloat16)
    temper = jnp.exp(logit_scale[0])
    offset = logit_bias[0]
    match_rows = pair_index.reshape(-1)
    key_list = []
    current = lax.all_gather(own_keys, "gather", axis=0, tiled=True)
    key_list.append(current)
    k = 1
    current = passed_along(current, "blk", 1)
    key_list.append(current)
    image_rows = lax.all_gather(queries, "gather", axis=0, tiled=True)
    block_rows = key_list[0].shape[0]
    columns = jnp.arange(block_rows, dtype=jnp.int32)
    image_grad = jnp.zeros((queries.shape[0], queries.shape[1]), jnp.float32)
    loss_total = jnp.zeros((), jnp.float32)
    scale_total = jnp.zeros((), jnp.float32)
    bias_total = jnp.zeros((), jnp.float32)
    caption_grad = jnp.zeros((own_keys.shape[0], own_keys.shape[1]), jnp.float32)
    for k in range(WINDOW):
        if k == 0:
            paired = columns[None, :] == match_rows[:, None]
        else:
            paired = jnp.zeros((queries.shape[0], block_rows), bool)
        loss_part, scale_part, bias_part, coeff_low = pair_terms(
            queries, key_list[k], temper, offset, paired
        )
        loss_total = loss_total + loss_part
        scale_total = scale_total + scale_part
        bias_total = bias_total + bias_part
        image_grad = image_grad + jnp.dot(
            coeff_low, key_list[k], preferred_element_type=jnp.float32
        )
        swapped = lax.all_to_all(coeff_low, "gather", split_axis=1, concat_axis=0, tiled=True)
        part = temper * key_partial(swapped, image_rows)
        if k > 0:
            part = passed_along(part, "blk", -k)
        caption_grad = caption_grad + part
    totals = lax.psum((loss_total, scale_total, bias_total), ("blk", "gather"))
    pair_count = block_rows * lax.axis_size("blk") * WINDOW * block_rows
    grad_images = backnorm(unit_img, inv_img, temper * image_grad)
    grad_captions = backnorm(unit_cap, inv_cap, caption_grad)
    loss_mean = (totals[0] / pair_count).reshape(1)
    grad_scale = (totals[1] / pair_count).reshape(1)
    grad_bias = (totals[2] / pair_count).reshape(1)
    return (loss_mean, grad_images, grad_captions, grad_scale, grad_bias)


def solution(mesh):
    placed = (P(("blk", "gather"), None), P(("blk", "gather"), None), P("blk", "gather"), P(), P())
    return jax.shard_map(
        on_device,
        mesh=mesh,
        in_specs=placed,
        out_specs=(P(), P(("blk", "gather"), None), P(("blk", "gather"), None), P(), P()),
        check_vma=False,
    )
```

profile of v0, /device:TPU:1, one launch (start us, length us, event | category | flops | bytes accessed | tf_op | source)
XLA Modules:
  0.0 382.7 jit_solution(350714610371364571)
XLA Ops:
  7.2 1.1 fusion.17
  8.3 1.8 fusion.6
  10.2 1.1 fusion.13
  11.3 1.8 fusion.9
  13.2 77.8 %all-gather.3.cloned.1.call-done = bf16[2048,1152]{1,0:T(8,128)(2,1)} async-done(((bf16[128,1152]{1,0:T(8,128)(2,1)}), bf16[2048,1152]{1,0:T(8,128)(2,1)}) %all-gather.3.cloned.1.call-update) | async-done | bytes 4718608 | tf_op jit(solution)/shard_map/all_gather | solution.py:54
  91.0 3.2 collective-permute-start
  95.5 4.1 %fusion.23 = f32[128,2048]{1,0:T(8,128)S(1)} fusion(bf16[128,1152]{1,0:T(8,128)(2,1)} %fusion.9, bf16[2048,1152]{1,0:T(8,128)(2,1)} %all-gather.3.cloned.1.call-done), kind=kOutput, calls=%fused_computation.45 | convolution fusion | flops 603979776 | bytes 6062080 | tf_op jit(solution)/shard_map/dot_general | solution.py:29
  99.6 2.1 fusion.22
  101.7 0.9 copy.17
  102.6 96.4 %collective-permute-done = bf16[2048,1152]{1,0:T(8,128)(2,1)S(1)} collective-permute-done((bf16[2048,1152]{1,0:T(8,128)(2,1)}, bf16[2048,1152]{1,0:T(8,128)(2,1)S(1)}, u32[]{:S(2)}, u32[]{:S(2)}) %collective-permute-start) | collective-permute-done | bytes 4718624 | tf_op jit(solution)/shard_map/ppermute | solution.py:15
  199.0 1.6 fusion.24
  201.2 1.6 fusion.21
  203.7 5.9 %all-to-all-start.1 = ((bf16[128,16,128]{2,0,1:T(8,128)(2,1)}), bf16[128,16,128]{2,0,1:T(8,128)(2,1)S(1)}, u32[]{:S(2)}, u32[]{:S(2)}) async-start(bf16[128,16,128]{2,0,1:T(8,128)(2,1)} %bitcast.30), calls=%async_computation.1 | async-start | bytes 1048576 | tf_op jit(solution)/shard_map/all_to_all | solution.py:81
  209.6 4.1 %fusion.19 = f32[128,1152]{1,0:T(8,128)} fusion(bf16[2048,1152]{1,0:T(8,128)(2,1)} %all-gather.3.cloned.1.call-done, f32[128,2048]{1,0:T(8,128)S(1)} %fusion.23, f32[]{:T(128)} %bitcast.34, f32[]{:T(128)} %bitcast.1, s32[128]{0:T(128)S(1)} %bitcast.39), kind=kOutput, calls=%fused_computation.39 | convolution fusion | flops 606339072 | bytes 6357512 | tf_op jit(solution)/shard_map/dot_general | solution.py:78
  217.7 3.3 all-to-all-done.1
  221.0 4.8 %all-to-all-start = ((bf16[128,16,128]{2,0,1:T(8,128)(2,1)}), bf16[128,16,128]{2,0,1:T(8,128)(2,1)S(1)}, u32[]{:S(2)}, u32[]{:S(2)}) async-start(bf16[128,16,128]{2,0,1:T(8,128)(2,1)} %bitcast.31), calls=%async_computation | async-start | bytes 1048576 | tf_op jit(solution)/shard_map/all_to_all | solution.py:81
  225.8 22.0 %all-gather.5.cloned.1.call-done = bf16[2048,1152]{1,0:T(8,128)(2,1)} async-done(((bf16[128,1152]{1,0:T(8,128)(2,1)}), bf16[2048,1152]{1,0:T(8,128)(2,1)}) %all-gather.5.cloned.1.call-update) | async-done | bytes 4718608 | tf_op jit(solution)/shard_map/all_gather | solution.py:59
  247.8 3.3 convolution_multiply_fusion
  251.1 5.1 %collective-permute-start.1 = (f32[128,1152]{1,0:T(8,128)S(1)}, f32[128,1152]{1,0:T(8,128)S(1)}, u32[]{:S(2)}, u32[]{:S(2)}) collective-permute-start(f32[128,1152]{1,0:T(8,128)S(1)} %convolution_multiply_fusion), channel_id=1, source_target_pairs={{16,0},{32,16},{48,32},{64,48},{80,64},{96,80},{112,96},{128,112},... | collective-permute-start | bytes 1769480 | tf_op jit(solution)/shard_map/ppermute | solution.py:15
  256.3 4.1 %fusion.10 = (f32[128]{0:T(128)S(1)}, f32[128,1152]{1,0:T(8,128)}) fusion(bf16[128,1152]{1,0:T(8,128)(2,1)S(1)} %copy-done.3, f32[128]{0:T(128)S(1)} %add_rsqrt_fusion.1, f32[128,1152]{1,0:T(8,128)S(1)} %copy-done.5, bf16[2048,1152]{1,0:T(8,128)(2,1)} %copy-done.2, f32[]{:T(128)} %bitcast.35, f32[128,2048]{1,0:T(8,128)S(1)} %fusion.24, f32[]{:T(128)} %bitcast.1), kind=kOutput, calls=%fused_computation.26 | convolution fusion | flops 606437248 | bytes 7242760 | tf_op jit(solution)/shard_map/dot_general | solution.py:78
  260.4 103.6 %all-reduce = (f32[]{:T(128)}, f32[]{:T(128)}, f32[]{:T(128)}) all-reduce(f32[]{:T(128)S(6)} %add.70, f32[]{:T(128)S(6)} %add.75, f32[]{:T(128)S(6)} %add.76), channel_id=1, replica_groups=mesh['blk'=32,'gather'=16] {'blk','gather'}, use_global_device_ids=true, to_apply=%region_4.5 | all-reduce | flops 3 | bytes 24 | tf_op jit(solution)/shard_map/psum | solution.py:86
  366.0 2.1 fusion.12
  368.1 3.3 fusion.14
  371.4 1.0 fusion.16
  (21 shorter events, 1.7 us)
Async XLA Ops:
  7.2 92.4 %copy-start.4 = (s32[1,128]{1,0:T(1,128)S(1)}, s32[1,128]{1,0:T(1,128)}, u32[]{:S(2)}) copy-start(s32[1,128]{1,0:T(1,128)} %param.7) | copy-start | bytes 1540
  7.2 83.8 %all-gather.3.cloned.1.call-start = ((), (), s32[]{:S(2)}) async-start(), calls=%async_computation.2 | async-start | bytes 5013504 | tf_op jit(solution)/shard_map/all_gather | solution.py:54
  10.2 237.7 %all-gather.5.cloned.1.call-start = ((), (), s32[]{:S(2)}) async-start(), calls=%async_computation.3 | async-start | bytes 5013504 | tf_op jit(solution)/shard_map/all_gather | solution.py:59
  13.1 185.8 %copy-start = (bf16[128,1152]{1,0:T(8,128)(2,1)S(1)}, bf16[128,1152]{1,0:T(8,128)(2,1)}, u32[]{:S(2)}) copy-start(bf16[128,1152]{1,0:T(8,128)(2,1)} %fusion.9) | copy-start | bytes 884740
  91.0 108.0 %collective-permute-start = (bf16[2048,1152]{1,0:T(8,128)(2,1)}, bf16[2048,1152]{1,0:T(8,128)(2,1)S(1)}, u32[]{:S(2)}, u32[]{:S(2)}) collective-permute-start(bf16[2048,1152]{1,0:T(8,128)(2,1)} %all-gather.3.cloned.1.call-done), channel_id=1, source_target_pairs={{496,0},{0,16},{16,32},{32,48},{48,64},{64,80},{80,96},{96,112},{1... | collective-permute-start | bytes 14155784 | tf_op jit(solution)/shard_map/ppermute | solution.py:15
  199.0 2.2 copy-start.2
  203.7 17.3 %all-to-all-start.1 = ((bf16[128,16,128]{2,0,1:T(8,128)(2,1)}), bf16[128,16,128]{2,0,1:T(8,128)(2,1)S(1)}, u32[]{:S(2)}, u32[]{:S(2)}) async-start(bf16[128,16,128]{2,0,1:T(8,128)(2,1)} %bitcast.30), calls=%async_computation.1 | async-start | bytes 1048576 | tf_op jit(solution)/shard_map/all_to_all | solution.py:81
  213.7 42.5 %copy-start.3 = (bf16[128,1152]{1,0:T(8,128)(2,1)S(1)}, bf16[128,1152]{1,0:T(8,128)(2,1)}, u32[]{:S(2)}) copy-start(bf16[128,1152]{1,0:T(8,128)(2,1)} %param.5) | copy-start | bytes 884740
  221.0 147.1 %all-to-all-start = ((bf16[128,16,128]{2,0,1:T(8,128)(2,1)}), bf16[128,16,128]{2,0,1:T(8,128)(2,1)S(1)}, u32[]{:S(2)}, u32[]{:S(2)}) async-start(bf16[128,16,128]{2,0,1:T(8,128)(2,1)} %bitcast.31), calls=%async_computation | async-start | bytes 1048576 | tf_op jit(solution)/shard_map/all_to_all | solution.py:81
  247.8 8.4 %copy-start.5 = (f32[128,1152]{1,0:T(8,128)S(1)}, f32[128,1152]{1,0:T(8,128)}, u32[]{:S(2)}) copy-start(f32[128,1152]{1,0:T(8,128)} %fusion.19) | copy-start | bytes 1769476
  251.1 117.0 %collective-permute-start.1 = (f32[128,1152]{1,0:T(8,128)S(1)}, f32[128,1152]{1,0:T(8,128)S(1)}, u32[]{:S(2)}, u32[]{:S(2)}) collective-permute-start(f32[128,1152]{1,0:T(8,128)S(1)} %convolution_multiply_fusion), channel_id=1, source_target_pairs={{16,0},{32,16},{48,32},{64,48},{80,64},{96,80},{112,96},{128,112},... | collective-permute-start | bytes 1769480 | tf_op jit(solution)/shard_map/ppermute | solution.py:15
  256.2 111.8 %copy-start.1 = (bf16[128,1152]{1,0:T(8,128)(2,1)S(1)}, bf16[128,1152]{1,0:T(8,128)(2,1)}, u32[]{:S(2)}) copy-start(bf16[128,1152]{1,0:T(8,128)(2,1)} %param.6) | copy-start | bytes 884740
Sparse Core Ops, SparseCore 0:
  11.9 79.0 all-gather.2
  94.3 153.5 all-gather.4
where the time goes:
time: 383 us
  waiting for transfers between devices  199 us (52%)
  blocking collectives  104 us (27%)
  between operations  24.8 us (6%)
  matrix products  20.6 us (5%)
  starting transfers between devices  19.1 us (5%)
  other arithmetic  12.6 us (3%)
    psum x1, blocking collectives, on_device(): totals = lax.psum((loss_total, scale_total, bias_total), ('blk', 'gather'))  104 us
    ppermute x2, waiting for transfers between devices, passed_along(): return lax.ppermute(block, axis, route)  96.4 us
    all_gather x1, waiting for transfers between devices, on_device(): current = lax.all_gather(own_keys, 'gather', axis=0, tiled=True)  77.8 us
    all_gather x1, waiting for transfers between devices, on_device(): image_rows = lax.all_gather(queries, 'gather', axis=0, tiled=True)  22 us
    all_to_all x2, starting transfers between devices, on_device(): lax.all_to_all(coeff_low, 'gather', split_axis=1, concat_axis=0, tiled=True)  10.7 us
    dot_general x2, matrix products, on_device(): jnp.dot(coeff_low, key_list[k], preferred_element_type=jnp.float32)  8.28 us
    ppermute x2, starting transfers between devices, passed_along(): return lax.ppermute(block, axis, route)  8.27 us
  transfers between devices with their start and end apart: 6, of which 4 were waited for; matrix products, arithmetic and copies ran while one was open for 7% of the time, Pallas kernels for 0%

commit v1 on v0

v1 whole, which is shorter than its diff:
```python
import functools

import jax
import jax.numpy as jnp
from jax import lax
from jax.experimental import pallas as pl
from jax.experimental.pallas import tpu as pltpu
from jax.sharding import PartitionSpec as P

MESH = pl.DeviceIdType.MESH
EPS = 1e-06
WINDOW = 2
NX = 4
ROWS = 128
E = 1152
LANES = 128

M_Q = 0
M_PI = 3
M_KSIB0, M_KY, M_KSIB1 = 6, 7, 8
M_KZ, M_KD, M_LSIB0, M_LSIB1 = 9, 10, 11, 12
M_DQ = 13
M_DQS = 16
M_SS = 19
M_Z, M_ZS, M_D, M_DS, M_Y, M_YS = 21, 22, 23, 24, 25, 26
M_ST = 27
N_MSG = 27 + 21


def kernel(n_blk, im_ref, cap_ref, pi_ref, ls_ref, lb_ref,
           loss_ref, gi_ref, gc_ref, gs_ref, gb_ref,
           Q, PI, K, C, S, INV, ACCQ, ACCK, SS, RS,
           SQ, SQS, RQ, RQS, SK, SKS, RK, RKS, ST, RT, SUMS,
           ssem, rsem):
    b = lax.axis_index("blk")
    g = lax.axis_index("gather")
    core = lax.rem(g, 2)
    x = lax.rem(g // 2, NX)
    yh = g // (2 * NX)
    nz = n_blk // 2
    zl_n = min(4, nz)
    zh_n = nz // zl_n
    z = lax.rem(b, nz)
    yl = b // nz
    zl = lax.rem(z, zl_n)
    zh = z // zl_n

    def gat(yh_, x_, core_):
        return yh_ * (2 * NX) + lax.rem(x_, NX) * 2 + core_

    def blk(yl_, zh_, zl_):
        return yl_ * nz + zh_ * zl_n + zl_

    g_off = [g, gat(yh, x + 2, core), gat(yh, x + 1, core), gat(yh, x + 3, core)]
    back = [0, 1, 3, 2]
    g_y = gat(1 - yh, x, core)
    b_n = lax.rem(b + 1, n_blk)
    b_p = lax.rem(b + n_blk - 1, n_blk)
    sib = (b, gat(yh, x, 1 - core))
    y_peer = (b, g_y)
    stage1 = []
    for i in range(1, 8):
        j = lax.rem(lax.rem(g, 8) + i, 8)
        stage1.append((b, yh * 8 + j))
    n2, n3 = 2 * zl_n, 2 * zh_n
    stage2 = []
    for i in range(1, n2):
        j = lax.rem(yh * zl_n + zl + i, n2)
        stage2.append((blk(yl, zh, lax.rem(j, zl_n)), gat(j // zl_n, x, core)))
    stage3 = []
    for i in range(1, n3):
        j = lax.rem(yl * zh_n + zh + i, n3)
        stage3.append((blk(j // zh_n, lax.rem(j, zh_n), zl), g))
    near = [(b_n, g), (b_p, g), (b_n, g_y), (b_p, g_y)]

    barrier = pltpu.get_barrier_semaphore()
    greeted = stage1 + stage2 + stage3 + near
    for peer in greeted:
        pl.semaphore_signal(barrier, inc=1, device_id=peer, device_id_type=MESH)

    def copy(m, src, dst, peer):
        return pltpu.make_async_remote_copy(
            src_ref=src, dst_ref=dst, send_sem=ssem.at[m], recv_sem=rsem.at[m],
            device_id=peer, device_id_type=MESH)

    temper = jnp.exp(jnp.full((1, LANES), ls_ref[0], jnp.float32))
    bias = lb_ref[0]
    PI[0] = jnp.broadcast_to(pi_ref[...], (8, LANES))

    def normalize(src, dst, which):
        def body(i, _):
            rows = pl.ds(pl.multiple_of(i * 16, 16), 16)
            v = src[rows, :].astype(jnp.float32)
            inv = lax.rsqrt(jnp.sum(v * v, axis=1, keepdims=True) + EPS)
            INV[which, rows, :] = jnp.broadcast_to(inv, (16, LANES))
            dst[rows, :] = (v * inv).astype(jnp.bfloat16)
            return 0
        lax.fori_loop(0, ROWS // 16, body, 0)

    normalize(im_ref, Q.at[0], 0)
    normalize(cap_ref, K.at[0, 0], 1)

    pl.semaphore_wait(barrier, len(greeted))

    sent = []

    def send(m, src, dst, peer):
        c = copy(m, src, dst, peer)
        c.start()
        sent.append(c)
        return c

    for s in (2, 3, 1):
        send(M_PI + s - 1, PI.at[0], PI.at[back[s]], (b, g_off[s]))
    for s in (2, 3, 1):
        send(M_Q + s - 1, Q.at[0], Q.at[back[s]], (b, g_off[s]))
    send(M_KY, K.at[0, 0], K.at[0, 1], y_peer)
    send(M_KZ, K.at[0, 0], K.at[1, 0], (b_n, g))
    send(M_KSIB0, K.at[0, 0], K.at[0, 2], sib)
    send(M_KD, K.at[0, 0], K.at[1, 1], (b_n, g_y))

    def arrived(m, dst):
        copy(m, dst, dst, sib).wait_recv()

    arrived(M_KY, K.at[0, 1])
    send(M_KSIB1, K.at[0, 1], K.at[0, 3], sib)
    arrived(M_KZ, K.at[1, 0])
    send(M_LSIB0, K.at[1, 0], K.at[1, 2], sib)
    arrived(M_KD, K.at[1, 1])
    send(M_LSIB1, K.at[1, 1], K.at[1, 3], sib)

    arrived(M_KSIB0, K.at[0, 2])
    arrived(M_KSIB1, K.at[0, 3])
    for s in (2, 3, 1):
        arrived(M_PI + back[s] - 1, PI.at[s])
        arrived(M_Q + back[s] - 1, Q.at[s])
    arrived(M_LSIB0, K.at[1, 2])
    arrived(M_LSIB1, K.at[1, 3])

    temper2 = jnp.concatenate([temper, temper], axis=1)
    k_base = [gat(yh, x, core), g_y, gat(yh, x, 1 - core), gat(1 - yh, x, 1 - core)]
    SUMS[...] = jnp.zeros_like(SUMS)
    NT = (((1,), (1,)), ((), ()))
    TN = (((0,), (0,)), ((), ()))

    def pair_terms(k, h):
        q2 = Q[2 * h:2 * h + 2].reshape(2 * ROWS, E)
        keys = K[k].reshape(4 * ROWS, E)
        S[...] = lax.dot_general(keys, q2, NT, preferred_element_type=jnp.float32)
        cols = slice(2 * h * ROWS, (2 * h + 2) * ROWS)
        pair = jnp.concatenate([PI[2 * h, 0:1], PI[2 * h + 1, 0:1]], axis=1)
        for t in range(4):
            def body(i, tot):
                rows = pl.ds(pl.multiple_of(t * ROWS + i * 32, 32), 32)
                ts = temper2 * S[rows, :]
                logits = ts + bias
                p = jnp.exp(logits)
                d = 1.0 + p
                coeff = p / d
                prod = (d[0:8] * d[8:16]) * (d[16:24] * d[24:32])
                loss = jnp.log(prod)
                if k == 0:
                    cid = lax.broadcasted_iota(jnp.int32, (32, 2 * ROWS), 0) + (k_base[t] * ROWS + i * 32)
                    hit = cid == pair
                    coeff = jnp.where(hit, coeff - 1.0, coeff)
                    own = jnp.where(hit, logits, 0.0)
                    loss = loss - ((own[0:8] + own[8:16]) + (own[16:24] + own[24:32]))
                sc = coeff * ts
                C[k, rows, cols] = coeff.astype(jnp.bfloat16)
                fold = lambda v: (v[0:8] + v[8:16]) + (v[16:24] + v[24:32])
                return tot[0] + loss, tot[1] + fold(sc), tot[2] + fold(coeff)
            zero = jnp.zeros((8, 2 * ROWS), jnp.float32)
            tot = lax.fori_loop(0, ROWS // 32, body, (zero, zero, zero))
            for j in range(3):
                SUMS[j] += tot[j]

    for h in range(2):
        for k in range(WINDOW):
            pair_terms(k, h)

    row = lax.broadcasted_iota(jnp.int32, (8, LANES), 0)
    mine = jnp.zeros((8, LANES), jnp.float32)
    for j in range(3):
        v = jnp.sum(SUMS[j], axis=0, keepdims=True)
        v = v[:, 0:LANES] + v[:, LANES:]
        mine = jnp.where(row == j, v, mine)
    ST[0] = mine
    for i, peer in enumerate(stage1):
        send(M_ST + i, ST.at[0], RT.at[0, i], peer)

    def quantize(src, srow, dst, dst_scale):
        def body(j, _):
            cs = pl.ds(pl.multiple_of(j * LANES, LANES), LANES)
            v = src[srow:srow + ROWS, cs]
            m = jnp.max(jnp.abs(v), axis=0, keepdims=True)
            up = 32767.0 / jnp.maximum(m, 1e-30)
            dst[:, cs] = jnp.round(v * up).astype(jnp.int32).astype(jnp.int16)
            dst_scale[:, cs] = m * (1.0 / 32767.0)
            return 0
        lax.fori_loop(0, E // LANES, body, 0)

    def image_part(h):
        cols = slice(2 * h * ROWS, (2 * h + 2) * ROWS)
        ACCQ[h] = (
            lax.dot_general(C[0, :, cols], K[0].reshape(4 * ROWS, E), TN, preferred_element_type=jnp.float32)
            + lax.dot_general(C[1, :, cols], K[1].reshape(4 * ROWS, E), TN, preferred_element_type=jnp.float32))

    def send_image(s):
        quantize(ACCQ.at[s // 2], (s % 2) * ROWS, SQ.at[s - 1], SQS.at[s - 1])
        send(M_DQ + s - 1, SQ.at[s - 1], RQ.at[back[s] - 1], (b, g_off[s]))
        send(M_DQS + s - 1, SQS.at[s - 1], RQS.at[back[s] - 1], (b, g_off[s]))

    def key_part(k, half):
        return jnp.dot(C[k, half * 256:half * 256 + 256, :], Q[...].reshape(4 * ROWS, E),
                       preferred_element_type=jnp.float32)

    SS[1] = key_part(1, 1)
    send(M_SS + 1, SS.at[1], RS.at[1], sib)
    image_part(1)
    send_image(2)
    send_image(3)
    ACCK[1] = key_part(1, 0)
    arrived(M_SS + 1, RS.at[1])

    def add_rs(k):
        def body(i, _):
            rows = pl.ds(pl.multiple_of(i * 16, 16), 16)
            ACCK[k, rows, :] += RS[k, rows, :]
            return 0
        lax.fori_loop(0, 2 * ROWS // 16, body, 0)

    def send_key(i, k, half, m, peer):
        quantize(ACCK.at[k], half * ROWS, SK.at[i], SKS.at[i])
        send(m, SK.at[i], RK.at[i], peer)
        send(m + 1, SKS.at[i], RKS.at[i], peer)

    add_rs(1)
    send_key(1, 1, 1, M_D, (b_p, g_y))
    send_key(0, 1, 0, M_Z, (b_p, g))
    image_part(0)
    send_image(1)
    SS[0] = key_part(0, 1)
    send(M_SS, SS.at[0], RS.at[0], sib)
    ACCK[0] = key_part(0, 0)
    arrived(M_SS, RS.at[0])
    add_rs(0)
    send_key(2, 0, 1, M_Y, y_peer)

    def gather_stage(st, peers, base):
        tot = ST[st]
        for i in range(len(peers)):
            arrived(M_ST + base + i, RT.at[st, i])
            tot = tot + RT[st, i]
        return tot

    tot = gather_stage(0, stage1, 0)
    ST[1] = tot
    for i, peer in enumerate(stage2):
        send(M_ST + 7 + i, ST.at[1], RT.at[1, i], peer)
    tot = gather_stage(1, stage2, 7)
    ST[2] = tot
    for i, peer in enumerate(stage3):
        send(M_ST + 14 + i, ST.at[2], RT.at[2, i], peer)
    tot = gather_stage(2, stage3, 14)
    count = 1.0 / (n_blk * WINDOW * 2048.0 * 2048.0)
    for j, ref in ((0, loss_ref), (1, gs_ref), (2, gb_ref)):
        ref[0] = jnp.sum(tot[j:j + 1, :]) * count

    def finish(src, which, own, parts, out):
        def body(i, _):
            rows = pl.ds(pl.multiple_of(i * 16, 16), 16)
            inv = INV[which, rows, 0:1]
            unit = src[rows, :].astype(jnp.float32) * inv
            grad = own[rows, :]
            for data, scale in parts:
                grad = grad + data[rows, :].astype(jnp.int32).astype(jnp.float32) * scale[...]
            grad = grad * temper[:, 0:1]
            along = jnp.sum(unit * grad, axis=1, keepdims=True)
            out[rows, :] = inv * (grad - unit * along)
            return 0
        lax.fori_loop(0, ROWS // 16, body, 0)

    for s in (2, 3, 1):
        arrived(M_DQ + back[s] - 1, RQ.at[s - 1])
        arrived(M_DQS + back[s] - 1, RQS.at[s - 1])
    finish(im_ref, 0, ACCQ.at[0], [(RQ.at[i], RQS.at[i]) for i in range(3)], gi_ref)
    for i, m in enumerate((M_Z, M_D, M_Y)):
        arrived(m, RK.at[i])
        arrived(m + 1, RKS.at[i])
    finish(cap_ref, 1, ACCK.at[0], [(RK.at[i], RKS.at[i]) for i in range(3)], gc_ref)
    for c in sent:
        c.wait_send()


def on_device(n_blk, images, captions, pair_index, logit_scale, logit_bias):
    vmem = pl.BlockSpec(memory_space=pltpu.VMEM)
    smem = pl.BlockSpec(memory_space=pltpu.SMEM)
    f32, bf16, i16 = jnp.float32, jnp.bfloat16, jnp.int16
    one = jax.ShapeDtypeStruct((1,), f32)
    grad = jax.ShapeDtypeStruct((ROWS, E), f32)
    unit = (ROWS, E)
    return pl.pallas_call(
        functools.partial(kernel, n_blk),
        out_shape=(one, grad, grad, one, one),
        in_specs=[vmem, vmem, vmem, smem, smem],
        out_specs=(smem, vmem, vmem, smem, smem),
        scratch_shapes=[
            pltpu.VMEM((4,) + unit, bf16),
            pltpu.VMEM((4, 8, LANES), jnp.int32),
            pltpu.VMEM((2, 4) + unit, bf16),
            pltpu.VMEM((2, 512, 512), bf16),
            pltpu.VMEM((512, 256), f32),
            pltpu.VMEM((2, ROWS, LANES), f32),
            pltpu.VMEM((2, 2 * ROWS, E), f32),
            pltpu.VMEM((2, 2 * ROWS, E), f32),
            pltpu.VMEM((2, 2 * ROWS, E), f32),
            pltpu.VMEM((2, 2 * ROWS, E), f32),
            pltpu.VMEM((3,) + unit, i16),
            pltpu.VMEM((3, 1, E), f32),
            pltpu.VMEM((3,) + unit, i16),
            pltpu.VMEM((3, 1, E), f32),
            pltpu.VMEM((3,) + unit, i16),
            pltpu.VMEM((3, 1, E), f32),
            pltpu.VMEM((3,) + unit, i16),
            pltpu.VMEM((3, 1, E), f32),
            pltpu.VMEM((3, 8, LANES), f32),
            pltpu.VMEM((3, 7, 8, LANES), f32),
            pltpu.VMEM((3, 8, 2 * LANES), f32),
            pltpu.SemaphoreType.DMA((N_MSG,)),
            pltpu.SemaphoreType.DMA((N_MSG,)),
        ],
        compiler_params=pltpu.CompilerParams(
            collective_id=0, has_side_effects=True, vmem_limit_bytes=48 * 2**20),
    )(images, captions, pair_index, logit_scale, logit_bias)


def solution(mesh):
    placed = (P(("blk", "gather"), None), P(("blk", "gather"), None), P("blk", "gather"), P(), P())
    return jax.shard_map(
        functools.partial(on_device, mesh.shape["blk"]),
        mesh=mesh,
        in_specs=placed,
        out_specs=(P(), P(("blk", "gather"), None), P(("blk", "gather"), None), P(), P()),
        check_vma=False,
    )
```

time: 383 us -> 82.4 us (0.22)
  the two profiles are of different devices: /device:TPU:1 before, /device:TPU:96 now
where the time goes in v1:
time: 82.4 us; the launch traced here: 82.1 us
  Pallas kernels  71.4 us (87%)
  between operations  7.14 us (9%)
  local copies, waits for them, and re-layouts  3.55 us (4%)
    pallas_call x1, Pallas kernels, on_device(): pl.pallas_call(functools.partial(kernel, n_blk), out_shape=(one, grad, gr...  71.4 us
    unnamed x8, local copies, waits for them, and re-layouts  3.55 us

profile of v1, /device:TPU:96, one launch (start us, length us, event | category | flops | bytes accessed | tf_op | source)
XLA Modules:
  0.0 82.1 jit_solution(4707384882714509287)
XLA Ops:
  1.3 0.0 copy-start.2
  1.9 0.0 copy-done.2
  2.0 0.0 copy-start
  2.0 1.0 %copy-done = bf16[128,1152]{1,0:T(8,128)(2,1)S(1)} copy-done((bf16[128,1152]{1,0:T(8,128)(2,1)S(1)}, bf16[128,1152]{1,0:T(8,128)(2,1)}, u32[]{:S(2)}) %copy-start) | copy-done | bytes 294936
  2.9 0.0 copy-start.1
  2.9 1.0 %copy-done.1 = bf16[128,1152]{1,0:T(8,128)(2,1)S(1)} copy-done((bf16[128,1152]{1,0:T(8,128)(2,1)S(1)}, bf16[128,1152]{1,0:T(8,128)(2,1)}, u32[]{:S(2)}) %copy-start.1) | copy-done | bytes 294936
  3.9 71.4 %shard_map.92 = (f32[1]{0:T(128)}, f32[128,1152]{1,0:T(8,128)S(1)}, f32[128,1152]{1,0:T(8,128)S(1)}, f32[1]{0:T(128)}, f32[1]{0:T(128)}) custom-call(bf16[128,1152]{1,0:T(8,128)(2,1)S(1)} %copy-done, bf16[128,1152]{1,0:T(8,128)(2,1)S(1)} %copy-done.1, s32[1,128]{1,0:T(1,128)S(1)} %copy-done.2, f32[1]{0:T(128)S(6)} %copy.15.ls_ref, f32[1]{0:T(128)S(6)} %copy.16.lb_ref), custom_call_target="tpu_custom_call" | custom-call | tf_op jit(solution)/shard_map/pallas_call | solution.py:302
  75.9 0.8 copy.18
  76.7 0.8 copy.19
Async XLA Ops:
  1.3 0.7 copy-start.2
  2.0 1.0 %copy-start = (bf16[128,1152]{1,0:T(8,128)(2,1)S(1)}, bf16[128,1152]{1,0:T(8,128)(2,1)}, u32[]{:S(2)}) copy-start(bf16[128,1152]{1,0:T(8,128)(2,1)} %im_ref.1) | copy-start | bytes 884740
  2.9 1.0 %copy-start.1 = (bf16[128,1152]{1,0:T(8,128)(2,1)S(1)}, bf16[128,1152]{1,0:T(8,128)(2,1)}, u32[]{:S(2)}) copy-start(bf16[128,1152]{1,0:T(8,128)(2,1)} %cap_ref.1) | copy-start | bytes 884740

commit v2 on v1

v2 whole, which is shorter than its diff:
```python
import functools

import jax
import jax.numpy as jnp
from jax import lax
from jax.experimental import pallas as pl
from jax.experimental.pallas import tpu as pltpu
from jax.sharding import PartitionSpec as P

MESH = pl.DeviceIdType.MESH
EPS = 1e-06
WINDOW = 2
NX = 4
ROWS = 128
E = 1152
LANES = 128

H = ROWS // 2

MESSAGES = [
    "QRa", "QRb", "QLb", "QLa", "QFR", "QFL", "PIR", "PIL", "PIO",
    "KYa", "KYb", "KZa", "KZb", "KS", "FZ", "FY", "S0a", "S0b", "S1a", "S1b", "S2a", "S2b",
    "XOa", "XOb", "XRa", "XRb", "XLa", "XLb", "Y1a", "Y0a", "Y0b", "Z1b", "Zob", "Zoa",
    "G1", "G0",
] + ["T%d%d" % (i, j) for i in range(3) for j in range(7)]
PARTS = ["XOa", "XOb", "XRa", "XRb", "XLa", "XLb", "Y1a", "Y0a", "Y0b", "Z1b", "Zob", "Zoa"]
SCALES = len(MESSAGES)
N_MSG = SCALES + len(PARTS)


def kernel(n_blk, im_hbm, cap_hbm, pi_ref, ls_ref, lb_ref,
           loss_ref, gi_ref, gc_ref, gs_ref, gb_ref,
           IM, CAP, Q, PI, K, C, INV, ACCQ, ACCK, SS, RS,
           SP, SPS, RP, RPS, ST, RT, SUMS, isem, ssem, rsem):
    b = lax.axis_index("blk")
    g = lax.axis_index("gather")
    core = lax.rem(g, 2)
    x = lax.rem(g // 2, NX)
    yh = g // (2 * NX)
    nz = n_blk // 2
    zl_n = min(4, nz)
    zh_n = nz // zl_n
    z = lax.rem(b, nz)
    yl = b // nz
    zl = lax.rem(z, zl_n)
    zh = z // zl_n

    def gat(yh_, x_, core_):
        return yh_ * (2 * NX) + lax.rem(x_, NX) * 2 + core_

    def blk(yl_, zh_, zl_):
        return yl_ * nz + zh_ * zl_n + zl_

    g_y = gat(1 - yh, x, core)
    right = (b, gat(yh, x + 1, core))
    left = (b, gat(yh, x + 3, core))
    opposite = (b, gat(yh, x + 2, core))
    b_n = lax.rem(b + 1, n_blk)
    b_p = lax.rem(b + n_blk - 1, n_blk)
    sib = (b, gat(yh, x, 1 - core))
    y_peer = (b, g_y)
    z_next = (b_n, g)
    z_prev = (b_p, g)
    stage1 = []
    for i in range(1, 8):
        j = lax.rem(lax.rem(g, 8) + i, 8)
        stage1.append((b, yh * 8 + j))
    n2, n3 = 2 * zl_n, 2 * zh_n
    stage2 = []
    for i in range(1, n2):
        j = lax.rem(yh * zl_n + zl + i, n2)
        stage2.append((blk(yl, zh, lax.rem(j, zl_n)), gat(j // zl_n, x, core)))
    stage3 = []
    for i in range(1, n3):
        j = lax.rem(yl * zh_n + zh + i, n3)
        stage3.append((blk(j // zh_n, lax.rem(j, zh_n), zl), g))

    barrier = pltpu.get_barrier_semaphore()
    greeted = stage1 + stage2 + stage3 + [z_next, z_prev]
    for peer in greeted:
        pl.semaphore_signal(barrier, inc=1, device_id=peer, device_id_type=MESH)

    fetch = [pltpu.make_async_copy(im_hbm, IM, isem.at[0]), pltpu.make_async_copy(cap_hbm, CAP, isem.at[1])]
    for f in fetch:
        f.start()

    temper = jnp.exp(jnp.full((1, LANES), ls_ref[0], jnp.float32))
    bias = lb_ref[0]
    PI[0] = jnp.broadcast_to(pi_ref[...], (8, LANES))
    SUMS[...] = jnp.zeros_like(SUMS)

    def normalize(src, dst, which):
        def body(i, _):
            rows = pl.ds(pl.multiple_of(i * 16, 16), 16)
            v = src[rows, :].astype(jnp.float32)
            inv = lax.rsqrt(jnp.sum(v * v, axis=1, keepdims=True) + EPS)
            INV[which, rows, :] = jnp.broadcast_to(inv, (16, LANES))
            dst[rows, :] = (v * inv).astype(jnp.bfloat16)
            return 0
        lax.fori_loop(0, ROWS // 16, body, 0, unroll=4)

    sent = []

    def copy(m, src, dst, peer):
        return pltpu.make_async_remote_copy(
            src_ref=src, dst_ref=dst, send_sem=ssem.at[m], recv_sem=rsem.at[m],
            device_id=peer, device_id_type=MESH)

    def send(name, src, dst, peer):
        m = name if isinstance(name, int) else MESSAGES.index(name)
        c = copy(m, src, dst, peer)
        c.start()
        sent.append(c)

    def arrived(name, dst):
        m = name if isinstance(name, int) else MESSAGES.index(name)
        copy(m, dst, dst, sib).wait_recv()

    a_half, b_half = pl.ds(0, H), pl.ds(H, H)
    OWN, LEFT, RIGHT, OPP = range(4)
    SIB, YP, YS = 1, 2, 3

    fetch[0].wait()
    normalize(IM, Q.at[OWN], 0)
    pl.semaphore_wait(barrier, len(greeted))
    send("PIR", PI.at[OWN], PI.at[LEFT], right)
    send("PIL", PI.at[OWN], PI.at[RIGHT], left)
    send("PIO", PI.at[OWN], PI.at[OPP], opposite)
    send("QRa", Q.at[OWN, a_half], Q.at[LEFT, a_half], right)
    send("QLb", Q.at[OWN, b_half], Q.at[RIGHT, b_half], left)
    send("QRb", Q.at[OWN, b_half], Q.at[LEFT, b_half], right)
    send("QLa", Q.at[OWN, a_half], Q.at[RIGHT, a_half], left)
    fetch[1].wait()
    normalize(CAP, K.at[0, OWN], 1)
    send("KYa", K.at[0, OWN, a_half], K.at[0, YP, a_half], y_peer)
    send("KZb", K.at[0, OWN, b_half], K.at[1, OWN, b_half], z_next)
    send("KYb", K.at[0, OWN, b_half], K.at[0, YP, b_half], y_peer)
    send("KZa", K.at[0, OWN, a_half], K.at[1, OWN, a_half], z_next)
    send("KS", K.at[0, OWN], K.at[0, SIB], sib)

    own_base = [gat(yh, x, core), gat(yh, x, 1 - core), g_y, gat(1 - yh, x, 1 - core)]
    NT = (((1,), (1,)), ((), ()))
    TN = (((0,), (0,)), ((), ()))

    def fold(v):
        return (v[0:8] + v[8:16]) + (v[16:24] + v[24:32])

    def pair_terms(k, kp, s):
        keys = K[k, 2 * kp:2 * kp + 2].reshape(2 * ROWS, E)
        sims = lax.dot_general(keys, Q[s], NT, preferred_element_type=jnp.float32)
        cols = slice(s * ROWS, (s + 1) * ROWS)
        tot = None
        for i in range(8):
            ts = temper * sims[i * 32:(i + 1) * 32]
            logits = ts + bias
            p = jnp.exp(logits)
            d = 1.0 + p
            coeff = p / d
            prod = (d[0:8] * d[8:16]) * (d[16:24] * d[24:32])
            loss = jnp.log(prod)
            t = 2 * kp + i // 4
            if k == 0:
                cid = lax.broadcasted_iota(jnp.int32, (32, ROWS), 0) + (own_base[t] * ROWS + (i % 4) * 32)
                hit = cid == PI[s, 0:1]
                coeff = jnp.where(hit, coeff - 1.0, coeff)
                loss = loss - fold(jnp.where(hit, logits, 0.0))
            C[k, t, (i % 4) * 32:(i % 4) * 32 + 32, cols] = coeff.astype(jnp.bfloat16)
            new = (loss, fold(coeff * ts), fold(coeff))
            tot = new if tot is None else tuple(u + v for u, v in zip(tot, new))
        for j in range(3):
            SUMS[j] += tot[j]

    arrived("KS", K.at[0, SIB])
    pair_terms(0, 0, OWN)

    arrived("QRa", Q.at[LEFT, a_half])
    send("QFR", Q.at[LEFT, a_half], Q.at[OPP, a_half], right)
    arrived("QLb", Q.at[RIGHT, b_half])
    send("QFL", Q.at[RIGHT, b_half], Q.at[OPP, b_half], left)
    arrived("KYa", K.at[0, YP, a_half])
    send("FZ", K.at[0, YP, a_half], K.at[1, YP, a_half], z_next)
    send("S0a", K.at[0, YP, a_half], K.at[0, YS, a_half], sib)
    arrived("KZb", K.at[1, OWN, b_half])
    send("FY", K.at[1, OWN, b_half], K.at[1, YP, b_half], y_peer)
    send("S1b", K.at[1, OWN, b_half], K.at[1, SIB, b_half], sib)
    arrived("KYb", K.at[0, YP, b_half])
    send("S0b", K.at[0, YP, b_half], K.at[0, YS, b_half], sib)
    arrived("KZa", K.at[1, OWN, a_half])
    send("S1a", K.at[1, OWN, a_half], K.at[1, SIB, a_half], sib)
    arrived("QRb", Q.at[LEFT, b_half])
    arrived("QLa", Q.at[RIGHT, a_half])
    arrived("PIR", PI.at[LEFT])
    arrived("PIL", PI.at[RIGHT])
    pair_terms(0, 0, LEFT)
    pair_terms(0, 0, RIGHT)
    arrived("S0a", K.at[0, YS, a_half])
    arrived("S0b", K.at[0, YS, b_half])
    for s in (OWN, LEFT, RIGHT):
        pair_terms(0, 1, s)
    arrived("FZ", K.at[1, YP, a_half])
    send("S2a", K.at[1, YP, a_half], K.at[1, YS, a_half], sib)
    arrived("FY", K.at[1, YP, b_half])
    send("S2b", K.at[1, YP, b_half], K.at[1, YS, b_half], sib)
    arrived("S1b", K.at[1, SIB, b_half])
    arrived("S1a", K.at[1, SIB, a_half])
    for s in (OWN, LEFT, RIGHT):
        pair_terms(1, 0, s)
    arrived("PIO", PI.at[OPP])
    arrived("QFR", Q.at[OPP, a_half])
    arrived("QFL", Q.at[OPP, b_half])
    pair_terms(1, 0, OPP)
    arrived("S2a", K.at[1, YS, a_half])
    arrived("S2b", K.at[1, YS, b_half])
    for s in (OWN, LEFT, RIGHT, OPP):
        pair_terms(1, 1, s)

    def key_part(k, slots):
        coeff = jnp.concatenate([C[k, t] for t in slots], axis=0)
        return jnp.dot(coeff, Q[...].reshape(4 * ROWS, E), preferred_element_type=jnp.float32)

    def image_part(slots):
        cols = slice(slots[0] * ROWS, (slots[-1] + 1) * ROWS)
        out = None
        for k in range(WINDOW):
            new = lax.dot_general(C[k, :, :, cols].reshape(4 * ROWS, -1), K[k].reshape(4 * ROWS, E), TN,
                                  preferred_element_type=jnp.float32)
            out = new if out is None else out + new
        for i, s in enumerate(slots):
            ACCQ[s] = out[i * ROWS:(i + 1) * ROWS]

    def part(name, terms, peer):
        p = PARTS.index(name)
        def body(j, _):
            cs = pl.ds(pl.multiple_of(j * LANES, LANES), LANES)
            v = None
            for t in terms:
                if isinstance(t, str):
                    q = PARTS.index(t)
                    u = RP[q, :, cs].astype(jnp.int32).astype(jnp.float32) * RPS[q, :, cs]
                else:
                    u = t[0][t[1], cs]
                v = u if v is None else v + u
            m = jnp.max(jnp.abs(v), axis=0, keepdims=True)
            up = 32767.0 / jnp.maximum(m, 1e-30)
            SP[p, :, cs] = jnp.round(v * up).astype(jnp.int32).astype(jnp.int16)
            SPS[p, :, cs] = m * (1.0 / 32767.0)
            return 0
        lax.fori_loop(0, E // LANES, body, 0, unroll=3)
        send(name, SP.at[p], RP.at[p], peer)
        send(SCALES + p, SPS.at[p], RPS.at[p], peer)

    def part_in(name):
        p = PARTS.index(name)
        arrived(name, RP.at[p])
        arrived(SCALES + p, RPS.at[p])

    SS[1] = key_part(1, (SIB, YS))
    send("G1", SS.at[1], RS.at[1], sib)
    pair_terms(0, 0, OPP)
    pair_terms(0, 1, OPP)

    row = lax.broadcasted_iota(jnp.int32, (8, LANES), 0)
    mine = jnp.zeros((8, LANES), jnp.float32)
    for j in range(3):
        mine = jnp.where(row == j, jnp.sum(SUMS[j], axis=0, keepdims=True), mine)
    ST[0] = mine
    for i, peer in enumerate(stage1):
        send("T0%d" % i, ST.at[0], RT.at[0, i], peer)

    def stage_sum(st, peers):
        tot = ST[st]
        for i in range(len(peers)):
            arrived("T%d%d" % (st, i), RT.at[st, i])
            tot = tot + RT[st, i]
        return tot

    image_part((OPP,))
    part("XOa", [(ACCQ.at[OPP], a_half)], right)
    part("XOb", [(ACCQ.at[OPP], b_half)], left)
    ACCK[1] = key_part(1, (OWN, YP))
    arrived("G1", RS.at[1])
    own_a, own_b, y_a, y_b = pl.ds(0, H), pl.ds(H, H), pl.ds(2 * H, H), pl.ds(3 * H, H)
    part("Y1a", [(ACCK.at[1], y_a), (RS.at[1], y_a)], y_peer)
    part("Z1b", [(ACCK.at[1], y_b), (RS.at[1], y_b)], z_prev)
    SS[0] = key_part(0, (SIB, YS))
    send("G0", SS.at[0], RS.at[0], sib)
    image_part((LEFT, RIGHT))
    part("XRb", [(ACCQ.at[RIGHT], b_half)], right)
    part("XLa", [(ACCQ.at[LEFT], a_half)], left)
    part("Zob", [(ACCK.at[1], own_b), (RS.at[1], own_b)], z_prev)
    ACCK[0] = key_part(0, (OWN, YP))
    arrived("G0", RS.at[0])
    part("Y0a", [(ACCK.at[0], y_a), (RS.at[0], y_a)], y_peer)

    ST[1] = stage_sum(0, stage1)
    for i, peer in enumerate(stage2):
        send("T1%d" % i, ST.at[1], RT.at[1, i], peer)

    part_in("XOa")
    part("XRa", [(ACCQ.at[RIGHT], a_half), "XOa"], right)
    part_in("XOb")
    part("XLb", [(ACCQ.at[LEFT], b_half), "XOb"], left)
    part_in("Y1a")
    part("Zoa", [(ACCK.at[1], own_a), (RS.at[1], own_a), "Y1a"], z_prev)
    part_in("Z1b")
    part("Y0b", [(ACCK.at[0], y_b), (RS.at[0], y_b), "Z1b"], y_peer)
    image_part((OWN,))

    ST[2] = stage_sum(1, stage2)
    for i, peer in enumerate(stage3):
        send("T2%d" % i, ST.at[2], RT.at[2, i], peer)

    def finish(half, src, which, own, parts, out):
        def body(i, _):
            local = pl.ds(pl.multiple_of(i * 16, 16), 16)
            rows = pl.ds(pl.multiple_of(half * H + i * 16, 16), 16)
            inv = INV[which, rows, 0:1]
            unit = src[rows, :].astype(jnp.float32) * inv
            grad = None
            for o in own:
                grad = o[rows, :] if grad is None else grad + o[rows, :]
            for name in parts:
                q = PARTS.index(name)
                grad = grad + RP[q, local, :].astype(jnp.int32).astype(jnp.float32) * RPS[q]
            grad = grad * temper[:, 0:1]
            along = jnp.sum(unit * grad, axis=1, keepdims=True)
            out[rows, :] = inv * (grad - unit * along)
            return 0
        lax.fori_loop(0, H // 16, body, 0, unroll=2)

    key_own = [ACCK.at[0], RS.at[0]]
    part_in("XRb")
    part_in("XLb")
    finish(1, IM, 0, [ACCQ.at[OWN]], ["XRb", "XLb"], gi_ref)
    part_in("XRa")
    part_in("XLa")
    finish(0, IM, 0, [ACCQ.at[OWN]], ["XRa", "XLa"], gi_ref)
    part_in("Zoa")
    part_in("Y0a")
    finish(0, CAP, 1, key_own, ["Zoa", "Y0a"], gc_ref)
    part_in("Zob")
    part_in("Y0b")
    finish(1, CAP, 1, key_own, ["Zob", "Y0b"], gc_ref)

    tot = stage_sum(2, stage3)
    count = 1.0 / (n_blk * WINDOW * 2048.0 * 2048.0)
    for j, ref in ((0, loss_ref), (1, gs_ref), (2, gb_ref)):
        ref[0] = jnp.sum(tot[j:j + 1, :]) * count
    for c in sent:
        c.wait_send()


def on_device(n_blk, images, captions, pair_index, logit_scale, logit_bias):
    vmem = pl.BlockSpec(memory_space=pltpu.VMEM)
    smem = pl.BlockSpec(memory_space=pltpu.SMEM)
    hbm = pl.BlockSpec(memory_space=pl.ANY)
    f32, bf16, i16 = jnp.float32, jnp.bfloat16, jnp.int16
    one = jax.ShapeDtypeStruct((1,), f32)
    grad = jax.ShapeDtypeStruct((ROWS, E), f32)
    unit = (ROWS, E)
    n = len(PARTS)
    return pl.pallas_call(
        functools.partial(kernel, n_blk),
        out_shape=(one, grad, grad, one, one),
        in_specs=[hbm, hbm, vmem, smem, smem],
        out_specs=(smem, vmem, vmem, smem, smem),
        scratch_shapes=[
            pltpu.VMEM(unit, bf16),
            pltpu.VMEM(unit, bf16),
            pltpu.VMEM((4,) + unit, bf16),
            pltpu.VMEM((4, 8, LANES), jnp.int32),
            pltpu.VMEM((2, 4) + unit, bf16),
            pltpu.VMEM((2, 4, ROWS, 4 * ROWS), bf16),
            pltpu.VMEM((2, ROWS, LANES), f32),
            pltpu.VMEM((4,) + unit, f32),
            pltpu.VMEM((2, 2 * ROWS, E), f32),
            pltpu.VMEM((2, 2 * ROWS, E), f32),
            pltpu.VMEM((2, 2 * ROWS, E), f32),
            pltpu.VMEM((n, H, E), i16),
            pltpu.VMEM((n, 1, E), f32),
            pltpu.VMEM((n, H, E), i16),
            pltpu.VMEM((n, 1, E), f32),
            pltpu.VMEM((3, 8, LANES), f32),
            pltpu.VMEM((3, 7, 8, LANES), f32),
            pltpu.VMEM((3, 8, LANES), f32),
            pltpu.SemaphoreType.DMA((2,)),
            pltpu.SemaphoreType.DMA((N_MSG,)),
            pltpu.SemaphoreType.DMA((N_MSG,)),
        ],
        compiler_params=pltpu.CompilerParams(
            collective_id=0, has_side_effects=True, vmem_limit_bytes=48 * 2**20),
    )(images, captions, pair_index, logit_scale, logit_bias)


def solution(mesh):
    placed = (P(("blk", "gather"), None), P(("blk", "gather"), None), P("blk", "gather"), P(), P())
    return jax.shard_map(
        functools.partial(on_device, mesh.shape["blk"]),
        mesh=mesh,
        in_specs=placed,
        out_specs=(P(), P(("blk", "gather"), None), P(("blk", "gather"), None), P(), P()),
        check_vma=False,
    )
```

time: 82.4 us -> 70.2 us (0.85)
  the two profiles are of different devices: /device:TPU:96 before, /device:TPU:1 now
where the time goes in v2:
time: 70.2 us; the launch traced here: 69.9 us
  Pallas kernels  59.2 us (84%)
  between operations  7.14 us (10%)
  local copies, waits for them, and re-layouts  3.55 us (5%)
    pallas_call x1, Pallas kernels, on_device(): pl.pallas_call(functools.partial(kernel, n_blk), out_shape=(one, grad, gr...  59.2 us
    unnamed x8, local copies, waits for them, and re-layouts  3.55 us

profile of v2, /device:TPU:1, one launch (start us, length us, event | category | flops | bytes accessed | tf_op | source)
XLA Modules:
  0.0 69.9 jit_solution(12288996105444355537)
XLA Ops:
  1.3 0.0 copy-start.2
  1.9 0.0 copy-done.2
  2.0 0.0 copy-start
  2.0 1.0 %copy-done = bf16[128,1152]{1,0:T(8,128)(2,1)S(1)} copy-done((bf16[128,1152]{1,0:T(8,128)(2,1)S(1)}, bf16[128,1152]{1,0:T(8,128)(2,1)}, u32[]{:S(2)}) %copy-start) | copy-done | bytes 294936
  2.9 0.0 copy-start.1
  2.9 1.0 %copy-done.1 = bf16[128,1152]{1,0:T(8,128)(2,1)S(1)} copy-done((bf16[128,1152]{1,0:T(8,128)(2,1)S(1)}, bf16[128,1152]{1,0:T(8,128)(2,1)}, u32[]{:S(2)}) %copy-start.1) | copy-done | bytes 294936
  3.9 59.2 %shard_map.92 = (f32[1]{0:T(128)}, f32[128,1152]{1,0:T(8,128)S(1)}, f32[128,1152]{1,0:T(8,128)S(1)}, f32[1]{0:T(128)}, f32[1]{0:T(128)}) custom-call(bf16[128,1152]{1,0:T(8,128)(2,1)S(1)} %copy-done, bf16[128,1152]{1,0:T(8,128)(2,1)S(1)} %copy-done.1, s32[1,128]{1,0:T(1,128)S(1)} %copy-done.2, f32[1]{0:T(128)S(6)} %copy.15.ls_ref, f32[1]{0:T(128)S(6)} %copy.16.lb_ref), custom_call_target="tpu_custom_call" | custom-call | tf_op jit(solution)/shard_map/pallas_call | solution.py:362
  63.7 0.8 %copy.18 = f32[128,1152]{1,0:T(8,128)} copy(f32[128,1152]{1,0:T(8,128)S(1)} %get-tuple-element.11) | data formatting | bytes 1179648
  64.5 0.8 %copy.19 = f32[128,1152]{1,0:T(8,128)} copy(f32[128,1152]{1,0:T(8,128)S(1)} %get-tuple-element.12) | data formatting | bytes 1179648
Async XLA Ops:
  1.3 0.7 copy-start.2
  2.0 1.0 %copy-start = (bf16[128,1152]{1,0:T(8,128)(2,1)S(1)}, bf16[128,1152]{1,0:T(8,128)(2,1)}, u32[]{:S(2)}) copy-start(bf16[128,1152]{1,0:T(8,128)(2,1)} %im_hbm.1) | copy-start | bytes 884740
  2.9 1.0 %copy-start.1 = (bf16[128,1152]{1,0:T(8,128)(2,1)S(1)}, bf16[128,1152]{1,0:T(8,128)(2,1)}, u32[]{:S(2)}) copy-start(bf16[128,1152]{1,0:T(8,128)(2,1)} %cap_hbm.1) | copy-start | bytes 884740

commit v3 on v2

--- a/solution.py
+++ b/solution.py
@@ -21,16 +21,16 @@
     "QRa", "QRb", "QLb", "QLa", "QFR", "QFL", "PIR", "PIL", "PIO",
     "KYa", "KYb", "KZa", "KZb", "KS", "FZ", "FY", "S0a", "S0b", "S1a", "S1b", "S2a", "S2b",
     "XOa", "XOb", "XRa", "XRb", "XLa", "XLb", "Y1a", "Y0a", "Y0b", "Z1b", "Zob", "Zoa",
-    "G1", "G0",
+    "G1y", "G1o", "G0y", "G0o", "DA", "DB", "Z1a", "EB",
 ] + ["T%d%d" % (i, j) for i in range(3) for j in range(7)]
-PARTS = ["XOa", "XOb", "XRa", "XRb", "XLa", "XLb", "Y1a", "Y0a", "Y0b", "Z1b", "Zob", "Zoa"]
+PARTS = ["XOa", "XOb", "XRa", "XRb", "XLa", "XLb", "Y1a", "Y0a", "Y0b", "Z1b", "Zob", "Zoa", "DA", "DB", "Z1a"]
 SCALES = len(MESSAGES)
 N_MSG = SCALES + len(PARTS)
 
 
-def kernel(n_blk, im_hbm, cap_hbm, pi_ref, ls_ref, lb_ref,
-           loss_ref, gi_ref, gc_ref, gs_ref, gb_ref,
-           IM, CAP, Q, PI, K, C, INV, ACCQ, ACCK, SS, RS,
+def kernel(n_blk, im_hbm, cap_hbm, pi_hbm, ls_ref, lb_ref,
+           loss_ref, GI, GC, gs_ref, gb_ref,
+           IM, CAP, PIN, Q, PI, K, C, INV, ACCQ, ACCK, SS, RS,
            SP, SPS, RP, RPS, ST, RT, SUMS, isem, ssem, rsem):
     b = lax.axis_index("blk")
     g = lax.axis_index("gather")
@@ -61,6 +61,12 @@
     y_peer = (b, g_y)
     z_next = (b_n, g)
     z_prev = (b_p, g)
+    first, last = z == 0, z == nz - 1
+    not_first, not_last = z != 0, z != nz - 1
+    inner = jnp.logical_and(not_first, not_last)
+    before_last, not_before_last = z == nz - 2, z != nz - 2
+    zy_next = (b_n, g_y)
+    zy_prev = (b_p, g_y)
     stage1 = []
     for i in range(1, 8):
         j = lax.rem(lax.rem(g, 8) + i, 8)
@@ -76,17 +82,17 @@
         stage3.append((blk(j // zh_n, lax.rem(j, zh_n), zl), g))
 
     barrier = pltpu.get_barrier_semaphore()
-    greeted = stage1 + stage2 + stage3 + [z_next, z_prev]
+    greeted = stage1 + stage2 + stage3 + [z_next, z_prev, zy_next, zy_prev]
     for peer in greeted:
         pl.semaphore_signal(barrier, inc=1, device_id=peer, device_id_type=MESH)
 
-    fetch = [pltpu.make_async_copy(im_hbm, IM, isem.at[0]), pltpu.make_async_copy(cap_hbm, CAP, isem.at[1])]
+    fetch = [pltpu.make_async_copy(im_hbm, IM, isem.at[0]), pltpu.make_async_copy(cap_hbm, CAP, isem.at[1]),
+             pltpu.make_async_copy(pi_hbm, PIN, isem.at[2])]
     for f in fetch:
         f.start()
 
     temper = jnp.exp(jnp.full((1, LANES), ls_ref[0], jnp.float32))
     bias = lb_ref[0]
-    PI[0] = jnp.broadcast_to(pi_ref[...], (8, LANES))
     SUMS[...] = jnp.zeros_like(SUMS)
 
     def normalize(src, dst, which):
@@ -101,25 +107,29 @@
 
     sent = []
 
-    def copy(m, src, dst, peer):
+    def number(name):
+        return name if isinstance(name, int) else MESSAGES.index(name)
+
+    def copy(m, src, dst, peer, r=None):
         return pltpu.make_async_remote_copy(
-            src_ref=src, dst_ref=dst, send_sem=ssem.at[m], recv_sem=rsem.at[m],
+            src_ref=src, dst_ref=dst, send_sem=ssem.at[number(m)], recv_sem=rsem.at[number(m if r is None else r)],
             device_id=peer, device_id_type=MESH)
 
-    def send(name, src, dst, peer):
-        m = name if isinstance(name, int) else MESSAGES.index(name)
-        c = copy(m, src, dst, peer)
+    def send(name, src, dst, peer, as_name=None, keep=True):
+        c = copy(name, src, dst, peer, as_name)
         c.start()
-        sent.append(c)
+        if keep:
+            sent.append(c)
 
     def arrived(name, dst):
-        m = name if isinstance(name, int) else MESSAGES.index(name)
-        copy(m, dst, dst, sib).wait_recv()
+        copy(name, dst, dst, sib).wait_recv()
 
     a_half, b_half = pl.ds(0, H), pl.ds(H, H)
     OWN, LEFT, RIGHT, OPP = range(4)
     SIB, YP, YS = 1, 2, 3
 
+    fetch[2].wait()
+    PI[0] = jnp.broadcast_to(PIN[...], (8, LANES))
     fetch[0].wait()
     normalize(IM, Q.at[OWN], 0)
     pl.semaphore_wait(barrier, len(greeted))
@@ -133,9 +143,21 @@
     fetch[1].wait()
     normalize(CAP, K.at[0, OWN], 1)
     send("KYa", K.at[0, OWN, a_half], K.at[0, YP, a_half], y_peer)
-    send("KZb", K.at[0, OWN, b_half], K.at[1, OWN, b_half], z_next)
+
+    @pl.when(last)
+    def _():
+        for i in range(H // 32):
+            for lo, same, other in ((H, "KZb", "EB"), (0, "KZa", "FZ")):
+                rows = pl.ds(lo + i * 32, 32)
+                send(same, K.at[0, OWN, rows], K.at[1, OWN, rows], z_next, keep=False)
+                send(other, K.at[0, OWN, rows], K.at[1, YP, rows], zy_next, "FY" if other == "EB" else None, keep=False)
+
+    @pl.when(not_last)
+    def _():
+        send("KZb", K.at[0, OWN, b_half], K.at[1, OWN, b_half], z_next, keep=False)
+        send("KZa", K.at[0, OWN, a_half], K.at[1, OWN, a_half], z_next, keep=False)
+
     send("KYb", K.at[0, OWN, b_half], K.at[0, YP, b_half], y_peer)
-    send("KZa", K.at[0, OWN, a_half], K.at[1, OWN, a_half], z_next)
     send("KS", K.at[0, OWN], K.at[0, SIB], sib)
 
     own_base = [gat(yh, x, core), gat(yh, x, 1 - core), g_y, gat(1 - yh, x, 1 - core)]
@@ -178,10 +200,18 @@
     arrived("QLb", Q.at[RIGHT, b_half])
     send("QFL", Q.at[RIGHT, b_half], Q.at[OPP, b_half], left)
     arrived("KYa", K.at[0, YP, a_half])
-    send("FZ", K.at[0, YP, a_half], K.at[1, YP, a_half], z_next)
+
+    @pl.when(not_last)
+    def _():
+        send("FZ", K.at[0, YP, a_half], K.at[1, YP, a_half], z_next, keep=False)
+
     send("S0a", K.at[0, YP, a_half], K.at[0, YS, a_half], sib)
     arrived("KZb", K.at[1, OWN, b_half])
-    send("FY", K.at[1, OWN, b_half], K.at[1, YP, b_half], y_peer)
+
+    @pl.when(not_first)
+    def _():
+        send("FY", K.at[1, OWN, b_half], K.at[1, YP, b_half], y_peer, keep=False)
+
     send("S1b", K.at[1, OWN, b_half], K.at[1, SIB, b_half], sib)
     arrived("KYb", K.at[0, YP, b_half])
     send("S0b", K.at[0, YP, b_half], K.at[0, YS, b_half], sib)
@@ -208,15 +238,26 @@
     arrived("PIO", PI.at[OPP])
     arrived("QFR", Q.at[OPP, a_half])
     arrived("QFL", Q.at[OPP, b_half])
+    pair_terms(0, 0, OPP)
+    pair_terms(0, 1, OPP)
+
+    def key_part(k, slots):
+        coeff = jnp.concatenate([C[k, t] for t in slots], axis=0)
+        return jnp.dot(coeff, Q[...].reshape(4 * ROWS, E), preferred_element_type=jnp.float32)
+
+    def swap(k):
+        rows = pl.ds(ROWS, ROWS)
+        SS[k] = key_part(k, (SIB, YS))
+        send("G%dy" % k, SS.at[k, rows], RS.at[k, rows], sib)
+        rows = pl.ds(0, ROWS)
+        send("G%do" % k, SS.at[k, rows], RS.at[k, rows], sib)
+
+    swap(0)
     pair_terms(1, 0, OPP)
     arrived("S2a", K.at[1, YS, a_half])
     arrived("S2b", K.at[1, YS, b_half])
     for s in (OWN, LEFT, RIGHT, OPP):
         pair_terms(1, 1, s)
-
-    def key_part(k, slots):
-        coeff = jnp.concatenate([C[k, t] for t in slots], axis=0)
-        return jnp.dot(coeff, Q[...].reshape(4 * ROWS, E), preferred_element_type=jnp.float32)
 
     def image_part(slots):
         cols = slice(slots[0] * ROWS, (slots[-1] + 1) * ROWS)
@@ -228,8 +269,9 @@
         for i, s in enumerate(slots):
             ACCQ[s] = out[i * ROWS:(i + 1) * ROWS]
 
-    def part(name, terms, peer):
+    def code(name, terms):
         p = PARTS.index(name)
+
         def body(j, _):
             cs = pl.ds(pl.multiple_of(j * LANES, LANES), LANES)
             v = None
@@ -246,18 +288,23 @@
             SPS[p, :, cs] = m * (1.0 / 32767.0)
             return 0
         lax.fori_loop(0, E // LANES, body, 0, unroll=3)
-        send(name, SP.at[p], RP.at[p], peer)
-        send(SCALES + p, SPS.at[p], RPS.at[p], peer)
+
+    def send_part(name, peer, to=None, keep=True):
+        p = PARTS.index(name)
+        q = p if to is None else PARTS.index(to)
+        send(name, SP.at[p], RP.at[q], peer, to, keep)
+        send(SCALES + p, SPS.at[p], RPS.at[q], peer, SCALES + q, keep)
+
+    def part(name, terms, peer):
+        code(name, terms)
+        send_part(name, peer)
 
     def part_in(name):
         p = PARTS.index(name)
         arrived(name, RP.at[p])
         arrived(SCALES + p, RPS.at[p])
 
-    SS[1] = key_part(1, (SIB, YS))
-    send("G1", SS.at[1], RS.at[1], sib)
-    pair_terms(0, 0, OPP)
-    pair_terms(0, 1, OPP)
+    swap(1)
 
     row = lax.broadcasted_iota(jnp.int32, (8, LANES), 0)
     mine = jnp.zeros((8, LANES), jnp.float32)
@@ -278,19 +325,61 @@
     part("XOa", [(ACCQ.at[OPP], a_half)], right)
     part("XOb", [(ACCQ.at[OPP], b_half)], left)
     ACCK[1] = key_part(1, (OWN, YP))
-    arrived("G1", RS.at[1])
+    arrived("G1y", RS.at[1, pl.ds(ROWS, ROWS)])
     own_a, own_b, y_a, y_b = pl.ds(0, H), pl.ds(H, H), pl.ds(2 * H, H), pl.ds(3 * H, H)
-    part("Y1a", [(ACCK.at[1], y_a), (RS.at[1], y_a)], y_peer)
-    part("Z1b", [(ACCK.at[1], y_b), (RS.at[1], y_b)], z_prev)
-    SS[0] = key_part(0, (SIB, YS))
-    send("G0", SS.at[0], RS.at[0], sib)
+    code("Y1a", [(ACCK.at[1], y_a), (RS.at[1], y_a)])
+
+    @pl.when(first)
+    def _():
+        send_part("Y1a", zy_prev, "DA", keep=False)
+
+    @pl.when(last)
+    def _():
+        send_part("Y1a", z_prev, "Z1a", keep=False)
+
+    @pl.when(inner)
+    def _():
+        send_part("Y1a", y_peer, keep=False)
+
+    arrived("G1o", RS.at[1, pl.ds(0, ROWS)])
+    zob = [(ACCK.at[1], own_b), (RS.at[1], own_b)]
+    zoa = [(ACCK.at[1], own_a), (RS.at[1], own_a)]
+
+    @pl.when(first)
+    def _():
+        code("Zob", zob)
+        send_part("Zob", z_prev, keep=False)
+
+    code("Z1b", [(ACCK.at[1], y_b), (RS.at[1], y_b)])
+
+    @pl.when(first)
+    def _():
+        send_part("Z1b", zy_prev, "DB", keep=False)
+        code("Zoa", zoa)
+        send_part("Zoa", z_prev, keep=False)
+
+    @pl.when(not_first)
+    def _():
+        send_part("Z1b", z_prev, keep=False)
+
     image_part((LEFT, RIGHT))
     part("XRb", [(ACCQ.at[RIGHT], b_half)], right)
     part("XLa", [(ACCQ.at[LEFT], a_half)], left)
-    part("Zob", [(ACCK.at[1], own_b), (RS.at[1], own_b)], z_prev)
+
+    @pl.when(not_first)
+    def _():
+        code("Zob", zob)
+        send_part("Zob", z_prev, keep=False)
+
     ACCK[0] = key_part(0, (OWN, YP))
-    arrived("G0", RS.at[0])
-    part("Y0a", [(ACCK.at[0], y_a), (RS.at[0], y_a)], y_peer)
+    arrived("G0y", RS.at[0, pl.ds(ROWS, ROWS)])
+    arrived("G0o", RS.at[0, pl.ds(0, ROWS)])
+    y0a = [(ACCK.at[0], y_a), (RS.at[0], y_a)]
+
+    @pl.when(not_before_last)
+    def _():
+        code("Y0a", y0a)
+        send_part("Y0a", y_peer, keep=False)
 
     ST[1] = stage_sum(0, stage1)
     for i, peer in enumerate(stage2):
@@ -300,10 +389,35 @@
     part("XRa", [(ACCQ.at[RIGHT], a_half), "XOa"], right)
     part_in("XOb")
     part("XLb", [(ACCQ.at[LEFT], b_half), "XOb"], left)
-    part_in("Y1a")
-    part("Zoa", [(ACCK.at[1], own_a), (RS.at[1], own_a), "Y1a"], z_prev)
-    part_in("Z1b")
-    part("Y0b", [(ACCK.at[0], y_b), (RS.at[0], y_b), "Z1b"], y_peer)
+    @pl.when(last)
+    def _():
+        code("Zoa", zoa)
+        send_part("Zoa", z_prev, keep=False)
+
+    @pl.when(inner)
+    def _():
+        part_in("Y1a")
+        code("Zoa", zoa + ["Y1a"])
+        send_part("Zoa", z_prev, keep=False)
+
+    y0b = [(ACCK.at[0], y_b), (RS.at[0], y_b)]
+
+    @pl.when(before_last)
+    def _():
+        part_in("Z1a")
+        code("Y0a", y0a + ["Z1a"])
+        send_part("Y0a", y_peer, keep=False)
+
+    @pl.when(last)
+    def _():
+        code("Y0b", y0b)
+
+    @pl.when(not_last)
+    def _():
+        part_in("Z1b")
+        code("Y0b", y0b + ["Z1b"])
+
+    send_part("Y0b", y_peer)
     image_part((OWN,))
 
     ST[2] = stage_sum(1, stage2)
@@ -331,16 +445,28 @@
     key_own = [ACCK.at[0], RS.at[0]]
     part_in("XRb")
     part_in("XLb")
-    finish(1, IM, 0, [ACCQ.at[OWN]], ["XRb", "XLb"], gi_ref)
+    finish(1, IM, 0, [ACCQ.at[OWN]], ["XRb", "XLb"], GI)
     part_in("XRa")
     part_in("XLa")
-    finish(0, IM, 0, [ACCQ.at[OWN]], ["XRa", "XLa"], gi_ref)
+    finish(0, IM, 0, [ACCQ.at[OWN]], ["XRa", "XLa"], GI)
     part_in("Zoa")
     part_in("Y0a")
-    finish(0, CAP, 1, key_own, ["Zoa", "Y0a"], gc_ref)
+
+    def finish_caption(half, names, extra):
+        @pl.when(last)
+        def _():
+            part_in(extra)
+            finish(half, CAP, 1, key_own, names + [extra], GC)
+
+        @pl.when(not_last)
+        def _():
+            finish(half, CAP, 1, key_own, names, GC)
+
+
+    finish_caption(0, ["Zoa", "Y0a"], "DA")
     part_in("Zob")
     part_in("Y0b")
-    finish(1, CAP, 1, key_own, ["Zob", "Y0b"], gc_ref)
+    finish_caption(1, ["Zob", "Y0b"], "DB")
 
     tot = stage_sum(2, stage3)
     count = 1.0 / (n_blk * WINDOW * 2048.0 * 2048.0)
@@ -348,12 +474,27 @@
         ref[0] = jnp.sum(tot[j:j + 1, :]) * count
     for c in sent:
         c.wait_send()
+    copy("FZ", K.at[0, OWN, a_half], K.at[1, YP, a_half], sib).wait_send()
+    copy("KZb", K.at[0, OWN, b_half], K.at[1, OWN, b_half], sib).wait_send()
+    copy("KZa", K.at[0, OWN, a_half], K.at[1, OWN, a_half], sib).wait_send()
+    for name in ("Y1a", "Z1b", "Y0a", "Zob", "Zoa"):
+        p = PARTS.index(name)
+        copy(name, SP.at[p], RP.at[p], sib).wait_send()
+        copy(SCALES + p, SPS.at[p], RPS.at[p], sib).wait_send()
+
+    @pl.when(last)
+    def _():
+        copy("EB", K.at[0, OWN, b_half], K.at[1, YP, b_half], zy_next, "FY").wait_send()
+
+    @pl.when(not_first)
+    def _():
+        copy("FY", K.at[1, OWN, b_half], K.at[1, YP, b_half], y_peer).wait_send()
 
 
 def on_device(n_blk, images, captions, pair_index, logit_scale, logit_bias):
+    smem = pl.BlockSpec(memory_space=pltpu.SMEM)
+    hbm = pl.BlockSpec(memory_space=pltpu.HBM)
     vmem = pl.BlockSpec(memory_space=pltpu.VMEM)
-    smem = pl.BlockSpec(memory_space=pltpu.SMEM)
-    hbm = pl.BlockSpec(memory_space=pl.ANY)
     f32, bf16, i16 = jnp.float32, jnp.bfloat16, jnp.int16
     one = jax.ShapeDtypeStruct((1,), f32)
     grad = jax.ShapeDtypeStruct((ROWS, E), f32)
@@ -362,11 +503,12 @@
     return pl.pallas_call(
         functools.partial(kernel, n_blk),
         out_shape=(one, grad, grad, one, one),
-        in_specs=[hbm, hbm, vmem, smem, smem],
+        in_specs=[hbm, hbm, hbm, smem, smem],
         out_specs=(smem, vmem, vmem, smem, smem),
         scratch_shapes=[
             pltpu.VMEM(unit, bf16),
             pltpu.VMEM(unit, bf16),
+            pltpu.VMEM((1, LANES), jnp.int32),
             pltpu.VMEM((4,) + unit, bf16),
             pltpu.VMEM((4, 8, LANES), jnp.int32),
             pltpu.VMEM((2, 4) + unit, bf16),
@@ -383,12 +525,12 @@
             pltpu.VMEM((3, 8, LANES), f32),
             pltpu.VMEM((3, 7, 8, LANES), f32),
             pltpu.VMEM((3, 8, LANES), f32),
-            pltpu.SemaphoreType.DMA((2,)),
+            pltpu.SemaphoreType.DMA((3,)),
             pltpu.SemaphoreType.DMA((N_MSG,)),
             pltpu.SemaphoreType.DMA((N_MSG,)),
         ],
         compiler_params=pltpu.CompilerParams(
-            collective_id=0, has_side_effects=True, vmem_limit_bytes=48 * 2**20),
+            collective_id=0, has_side_effects=True, vmem_limit_bytes=60 * 2**20),
     )(images, captions, pair_index, logit_scale, logit_bias)
 
 

time: 70.2 us -> 67.6 us (0.963)
  Pallas kernels: 59.2 us -> 57.4 us
  local copies, waits for them, and re-layouts: 3.55 us -> 2.8 us
    pallas_call x1, Pallas kernels: 59.2 us -> 57.4 us  [on_device(): pl.pallas_call(functools.partial(kernel, n_blk), out_shape=(one, grad, gr...]
    unnamed x8 -> x4, local copies, waits for them, and re-layouts: 3.55 us -> 2.8 us
where the time goes in v3:
time: 67.6 us; the launch traced here: 67.4 us
  Pallas kernels  57.4 us (85%)
  between operations  7.13 us (11%)
  local copies, waits for them, and re-layouts  2.8 us (4%)
    pallas_call x1, Pallas kernels, on_device(): pl.pallas_call(functools.partial(kernel, n_blk), out_shape=(one, grad, gr...  57.4 us
    unnamed x4, local copies, waits for them, and re-layouts  2.8 us

profile of v3, /device:TPU:1, one launch (start us, length us, event | category | flops | bytes accessed | tf_op | source)
XLA Modules:
  0.0 67.4 jit_solution(8085748064413752165)
XLA Ops:
  1.9 57.4 %shard_map.92 = (f32[1]{0:T(128)}, f32[128,1152]{1,0:T(8,128)}, f32[128,1152]{1,0:T(8,128)}, f32[1]{0:T(128)}, f32[1]{0:T(128)}) custom-call(bf16[128,1152]{1,0:T(8,128)(2,1)} %im_hbm.1, bf16[128,1152]{1,0:T(8,128)(2,1)} %cap_hbm.1, s32[1,128]{1,0:T(1,128)} %pi_hbm.1, f32[1]{0:T(128)S(6)} %copy.15.ls_ref, f32[1]{0:T(128)S(6)} %copy.16.lb_ref), custom_call_target="tpu_custom_call" | custom-call | tf_op jit(solution)/shard_map/pallas_call | solution.py:503
  60.0 0.0 copy-start
  60.0 2.0 %copy.18 = f32[128,1152]{1,0:T(8,128)} copy(f32[128,1152]{1,0:T(8,128)} %get-tuple-element.11) | data formatting | bytes 1179648
  62.0 0.0 copy-done
  62.0 0.8 %copy.19 = f32[128,1152]{1,0:T(8,128)} copy(f32[128,1152]{1,0:T(8,128)S(1)} %copy-done) | data formatting | bytes 1179648
Async XLA Ops:
  60.0 2.0 %copy-start = (f32[128,1152]{1,0:T(8,128)S(1)}, f32[128,1152]{1,0:T(8,128)}, u32[]{:S(2)}) copy-start(f32[128,1152]{1,0:T(8,128)} %get-tuple-element.12) | copy-start | bytes 1769476

commit v4 on v3

--- a/solution.py
+++ b/solution.py
@@ -130,9 +130,29 @@
 
     fetch[2].wait()
     PI[0] = jnp.broadcast_to(PIN[...], (8, LANES))
+    fetch[1].wait()
+    normalize(CAP, K.at[0, OWN], 1)
+    pl.semaphore_wait(barrier, len(greeted))
+    send("KYa", K.at[0, OWN, a_half], K.at[0, YP, a_half], y_peer)
+
+    @pl.when(last)
+    def _():
+        for i in range(H // 32):
+            for lo, same, other in ((H, "KZb", "EB"), (0, "KZa", "FZ")):
+                rows = pl.ds(lo + i * 32, 32)
+                send(same, K.at[0, OWN, rows], K.at[1, OWN, rows], z_next, keep=False)
+                send(other, K.at[0, OWN, rows], K.at[1, YP, rows], zy_next, "FY" if other == "EB" else None, keep=False)
+
+    @pl.when(not_last)
+    def _():
+        send("KZb", K.at[0, OWN, b_half], K.at[1, OWN, b_half], z_next, keep=False)
+        send("KZa", K.at[0, OWN, a_half], K.at[1, OWN, a_half], z_next, keep=False)
+
+    send("KYb", K.at[0, OWN, b_half], K.at[0, YP, b_half], y_peer)
+    send("KS", K.at[0, OWN], K.at[0, SIB], sib)
+
     fetch[0].wait()
     normalize(IM, Q.at[OWN], 0)
-    pl.semaphore_wait(barrier, len(greeted))
     send("PIR", PI.at[OWN], PI.at[LEFT], right)
     send("PIL", PI.at[OWN], PI.at[RIGHT], left)
     send("PIO", PI.at[OWN], PI.at[OPP], opposite)
@@ -140,25 +160,6 @@
     send("QLb", Q.at[OWN, b_half], Q.at[RIGHT, b_half], left)
     send("QRb", Q.at[OWN, b_half], Q.at[LEFT, b_half], right)
     send("QLa", Q.at[OWN, a_half], Q.at[RIGHT, a_half], left)
-    fetch[1].wait()
-    normalize(CAP, K.at[0, OWN], 1)
-    send("KYa", K.at[0, OWN, a_half], K.at[0, YP, a_half], y_peer)
-
-    @pl.when(last)
-    def _():
-        for i in range(H // 32):
-            for lo, same, other in ((H, "KZb", "EB"), (0, "KZa", "FZ")):
-                rows = pl.ds(lo + i * 32, 32)
-                send(same, K.at[0, OWN, rows], K.at[1, OWN, rows], z_next, keep=False)
-                send(other, K.at[0, OWN, rows], K.at[1, YP, rows], zy_next, "FY" if other == "EB" else None, keep=False)
-
-    @pl.when(not_last)
-    def _():
-        send("KZb", K.at[0, OWN, b_half], K.at[1, OWN, b_half], z_next, keep=False)
-        send("KZa", K.at[0, OWN, a_half], K.at[1, OWN, a_half], z_next, keep=False)
-
-    send("KYb", K.at[0, OWN, b_half], K.at[0, YP, b_half], y_peer)
-    send("KS", K.at[0, OWN], K.at[0, SIB], sib)
 
     own_base = [gat(yh, x, core), gat(yh, x, 1 - core), g_y, gat(1 - yh, x, 1 - core)]
     NT = (((1,), (1,)), ((), ()))
@@ -436,7 +437,6 @@
             for name in parts:
                 q = PARTS.index(name)
                 grad = grad + RP[q, local, :].astype(jnp.int32).astype(jnp.float32) * RPS[q]
-            grad = grad * temper[:, 0:1]
             along = jnp.sum(unit * grad, axis=1, keepdims=True)
             out[rows, :] = inv * (grad - unit * along)
             return 0
@@ -500,7 +500,7 @@
     grad = jax.ShapeDtypeStruct((ROWS, E), f32)
     unit = (ROWS, E)
     n = len(PARTS)
-    return pl.pallas_call(
+    loss, grad_images, grad_captions, grad_scale, grad_bias = pl.pallas_call(
         functools.partial(kernel, n_blk),
         out_shape=(one, grad, grad, one, one),
         in_specs=[hbm, hbm, hbm, smem, smem],
@@ -532,6 +532,8 @@
         compiler_params=pltpu.CompilerParams(
             collective_id=0, has_side_effects=True, vmem_limit_bytes=60 * 2**20),
     )(images, captions, pair_index, logit_scale, logit_bias)
+    temper = jnp.exp(logit_scale[0])
+    return loss, temper * grad_images, temper * grad_captions, grad_scale, grad_bias
 
 
 def solution(mesh):

time: 67.6 us -> 66.9 us (0.990)
  local copies, waits for them, and re-layouts: 2.8 us -> 0 us
  other arithmetic: 0 us -> 2.33 us
    unnamed x4 -> x0, local copies, waits for them, and re-layouts: 2.8 us -> none
    mul x0 -> x1, other arithmetic: none -> 2.33 us  [on_device(): temper * grad_captions]
where the time goes in v4:
time: 66.9 us; the launch traced here: 66.7 us
  Pallas kernels  57.2 us (86%)
  between operations  7.16 us (11%)
  other arithmetic  2.33 us (3%)
    pallas_call x1, Pallas kernels, on_device(): pl.pallas_call(functools.partial(kernel, n_blk), out_shape=(one, grad, gr...  57.2 us
    mul x1, other arithmetic, on_device(): temper * grad_captions  2.33 us

profile of v4, /device:TPU:1, one launch (start us, length us, event | category | flops | bytes accessed | tf_op | source)
XLA Modules:
  0.0 66.7 jit_solution(12461424733857093627)
XLA Ops:
  2.0 57.2 %shard_map.92 = (f32[1]{0:T(128)}, f32[128,1152]{1,0:T(8,128)}, f32[128,1152]{1,0:T(8,128)}, f32[1]{0:T(128)}, f32[1]{0:T(128)}) custom-call(bf16[128,1152]{1,0:T(8,128)(2,1)} %im_hbm.1, bf16[128,1152]{1,0:T(8,128)(2,1)} %cap_hbm.1, s32[1,128]{1,0:T(1,128)} %pi_hbm.1, f32[1]{0:T(128)S(6)} %copy.13.ls_ref, f32[1]{0:T(128)S(6)} %copy.14.lb_ref), custom_call_target="tpu_custom_call" | custom-call | tf_op jit(solution)/shard_map/pallas_call | solution.py:503
  59.2 2.3 %broadcast_multiply_fusion = (f32[128,1152]{1,0:T(8,128)}, f32[128,1152]{1,0:T(8,128)}) fusion(f32[128,1152]{1,0:T(8,128)} %get-tuple-element.12, f32[]{:T(128)} %bitcast, f32[128,1152]{1,0:T(8,128)} %get-tuple-element.11), kind=kLoop, calls=%fused_computation | loop fusion | flops 294912 | bytes 2359300 | tf_op jit(solution)/shard_map/mul | solution.py:536

commit v5 on v4

--- a/solution.py
+++ b/solution.py
@@ -296,6 +296,15 @@
         send(name, SP.at[p], RP.at[q], peer, to, keep)
         send(SCALES + p, SPS.at[p], RPS.at[q], peer, SCALES + q, keep)
 
+    def send_two(name, to, other):
+        p, q, r = PARTS.index(name), PARTS.index(to), PARTS.index(other)
+        for lo in range(0, H, 32):
+            rows = pl.ds(lo, 32)
+            send(name, SP.at[p, rows], RP.at[q, rows], zy_prev, to, False)
+            send(other, SP.at[r, rows], RP.at[r, rows], z_prev, None, False)
+        send(SCALES + p, SPS.at[p], RPS.at[q], zy_prev, SCALES + q, False)
+        send(SCALES + r, SPS.at[r], RPS.at[r], z_prev, None, False)
+
     def part(name, terms, peer):
         code(name, terms)
         send_part(name, peer)
@@ -330,10 +339,6 @@
     own_a, own_b, y_a, y_b = pl.ds(0, H), pl.ds(H, H), pl.ds(2 * H, H), pl.ds(3 * H, H)
     code("Y1a", [(ACCK.at[1], y_a), (RS.at[1], y_a)])
 
-    @pl.when(first)
-    def _():
-        send_part("Y1a", zy_prev, "DA", keep=False)
-
     @pl.when(last)
     def _():
         send_part("Y1a", z_prev, "Z1a", keep=False)
@@ -349,15 +354,14 @@
     @pl.when(first)
     def _():
         code("Zob", zob)
-        send_part("Zob", z_prev, keep=False)
+        send_two("Y1a", "DA", "Zob")
 
     code("Z1b", [(ACCK.at[1], y_b), (RS.at[1], y_b)])
 
     @pl.when(first)
     def _():
-        send_part("Z1b", zy_prev, "DB", keep=False)
         code("Zoa", zoa)
-        send_part("Zoa", z_prev, keep=False)
+        send_two("Z1b", "DB", "Zoa")
 
     @pl.when(not_first)
     def _():

time: 66.9 us -> 67.2 us (level)
  no operation moved by 1% of the time
where the time goes in v5:
time: 67.2 us; the launch traced here: 67 us
  Pallas kernels  57.5 us (86%)
  between operations  7.16 us (11%)
  other arithmetic  2.33 us (3%)
    pallas_call x1, Pallas kernels, on_device(): pl.pallas_call(functools.partial(kernel, n_blk), out_shape=(one, grad, gr...  57.5 us
    mul x1, other arithmetic, on_device(): temper * grad_captions  2.33 us

profile of v5, /device:TPU:1, one launch (start us, length us, event | category | flops | bytes accessed | tf_op | source)
XLA Modules:
  0.0 67.0 jit_solution(12061727731587424606)
XLA Ops:
  2.0 57.5 %shard_map.92 = (f32[1]{0:T(128)}, f32[128,1152]{1,0:T(8,128)}, f32[128,1152]{1,0:T(8,128)}, f32[1]{0:T(128)}, f32[1]{0:T(128)}) custom-call(bf16[128,1152]{1,0:T(8,128)(2,1)} %im_hbm.1, bf16[128,1152]{1,0:T(8,128)(2,1)} %cap_hbm.1, s32[1,128]{1,0:T(1,128)} %pi_hbm.1, f32[1]{0:T(128)S(6)} %copy.13.ls_ref, f32[1]{0:T(128)S(6)} %copy.14.lb_ref), custom_call_target="tpu_custom_call" | custom-call | tf_op jit(solution)/shard_map/pallas_call | solution.py:507
  59.5 2.3 %broadcast_multiply_fusion = (f32[128,1152]{1,0:T(8,128)}, f32[128,1152]{1,0:T(8,128)}) fusion(f32[128,1152]{1,0:T(8,128)} %get-tuple-element.12, f32[]{:T(128)} %bitcast, f32[128,1152]{1,0:T(8,128)} %get-tuple-element.11), kind=kLoop, calls=%fused_computation | loop fusion | flops 294912 | bytes 2359300 | tf_op jit(solution)/shard_map/mul | solution.py:540
